TPU v7x, 32 devices: a whole 2x2x4 slice. The times are simulated.
32 devices in a mesh: ctx: 8 (over z, y), wt: 4 (over x, core).
Axes of the slice: x: 2, y: 2, z: 4, core: 2. Of those that a mesh axis runs over, the one named last changes fastest.
Arguments:
- frames: bfloat16 [512, 1280], P('wt'), may hold values from -6 to 6
- span_source: int32 [32], P('wt'), may hold values from 0 to 7, as said below
- adapter_weight: bfloat16 [1280, 4096], P(None, 'ctx'), may hold values from -0.15625 to 0.15625
- adapter_bias: float32 [4096], P('ctx'), may hold values from -3 to 3
- norm_gain: float32 [4096], replicated, may hold values from 0.25 to 1.75
- qkv_weight: bfloat16 [4096, 3, 4096], P('wt', None, 'ctx'), may hold values from -0.09375 to 0.09375
- out_weight: bfloat16 [4096, 4096], P('ctx', 'wt'), may hold values from -0.125 to 0.125
- k_cache: bfloat16 [8, 1024, 4096], P('wt', 'ctx'), may hold values from -600 to 600
- v_cache: bfloat16 [8, 1024, 4096], P('wt', 'ctx'), may hold values from -12 to 12
- lengths: int32 [8], P('wt'), may hold values from 1 to 1024
Outputs:
- attn_out: bfloat16 [512, 4096], P('wt', 'ctx')
- new_keys: bfloat16 [512, 4096], P('wt', 'ctx')
- new_values: bfloat16 [512, 4096], P('wt', 'ctx')
Inputs may be any that keep to these rules, and one draw needn't show every extreme that they name: `span_source`: each aligned block of 8 entries is a permutation of 0 to 7.
All inputs are finite; a program needn't handle non-finite values.
Results may differ from a plain program's by a relative error of at most 0.02.
Values may be sent and summed in bfloat16 or wider, within the bound.
A program may use at most 64 MiB of HBM per device.

v0:
```python
import jax
import jax.numpy as jnp
from jax import lax
from jax.sharding import PartitionSpec as P

HEADS = 32
HEAD = 128


FLOOR_SCORE = -1e30


def rotate(values, positions):
    half = values.shape[-1] // 2
    freq = 10000.0 ** (-2.0 * jnp.arange(half, dtype=jnp.float32) / values.shape[-1])
    angle = positions.astype(jnp.float32)[:, None] * freq[None, :]
    cosine = jnp.cos(angle)[:, None, :]
    sine = jnp.sin(angle)[:, None, :]
    first = values[..., :half]
    second = values[..., half:]
    return jnp.concatenate(
        [first * cosine - second * sine, second * cosine + first * sine], axis=-1
    )


def combine_parts(left, right):
    left_max, left_total, left_numer = left
    right_max, right_total, right_numer = right
    joint = jnp.maximum(left_max, right_max)
    left_scale = jnp.exp(left_max - joint)
    right_scale = jnp.exp(right_max - joint)
    return (
        joint,
        left_total * left_scale + right_total * right_scale,
        left_numer * left_scale[..., None] + right_numer * right_scale[..., None],
    )


def finish_heads(parts):
    shard_max, shard_total, shard_numer = parts
    joint = jnp.max(shard_max, axis=0)
    factor = jnp.exp(shard_max - joint[None])
    total = jnp.sum(shard_total * factor, axis=0)
    numer = jnp.sum(shard_numer * factor[..., None], axis=0)
    return (numer / total[..., None]).astype(jnp.bfloat16)


def shards(
    frames,
    span_source,
    adapter_weight,
    adapter_bias,
    norm_gain,
    qkv_weight,
    out_weight,
    k_cache,
    v_cache,
    lengths,
):
    tok_rows, audio_width = frames.shape
    group_spans = span_source.shape[0]
    span_len = tok_rows // group_spans
    meet_count = lengths.shape[0]
    new_count = tok_rows // meet_count
    hist_local = k_cache.shape[1]
    cols_local = qkv_weight.shape[2]
    heads_here = cols_local // HEAD
    scale = HEAD ** (-0.5)
    ctx_rank = lax.axis_index("ctx")
    head_start = ctx_rank * heads_here
    ordered = frames.reshape(group_spans, span_len, audio_width)[span_source].reshape(
        tok_rows, audio_width
    )
    adapted = (
        jnp.dot(ordered, adapter_weight, preferred_element_type=jnp.float32) + adapter_bias
    ).astype(jnp.bfloat16)
    features = lax.all_gather(adapted, "ctx", axis=1, tiled=True)
    wide = features.astype(jnp.float32)
    normed = (
        wide * lax.rsqrt(jnp.mean(wide * wide, axis=-1, keepdims=True) + 1e-06) * norm_gain
    ).astype(jnp.bfloat16)
    qkv_full, out_rows = (
        lax.all_gather(qkv_weight, "wt", axis=0, tiled=True),
        lax.all_gather(out_weight, "wt", axis=1, tiled=True),
    )
    projected = jnp.einsum("rd,dke->rke", normed, qkv_full, preferred_element_type=jnp.float32)
    positions = (lengths[:, None] + jnp.arange(new_count, dtype=jnp.int32)[None, :]).reshape(
        tok_rows
    )
    query_local = rotate(projected[:, 0].reshape(tok_rows, heads_here, HEAD), positions).astype(
        jnp.bfloat16
    )
    key_local = rotate(projected[:, 1].reshape(tok_rows, heads_here, HEAD), positions).astype(
        jnp.bfloat16
    )
    value_local = projected[:, 2].reshape(tok_rows, heads_here, HEAD).astype(jnp.bfloat16)
    query_every = lax.all_gather(
        query_local.reshape(tok_rows, cols_local), "ctx", axis=1, tiled=True
    )
    query_heads = query_every.reshape(meet_count, new_count, HEADS, HEAD)
    keys_hist = k_cache.reshape(meet_count, hist_local, HEADS, HEAD)
    vals_hist = v_cache.reshape(meet_count, hist_local, HEADS, HEAD)
    scores = (
        jnp.einsum("mthd,mphd->mhtp", query_heads, keys_hist, preferred_element_type=jnp.float32)
        * scale
    )
    key_place = ctx_rank * hist_local + jnp.arange(hist_local, dtype=jnp.int32)
    live = (key_place[None, :] < lengths[:, None])[:, None, None, :]
    hist_max = jnp.maximum(jnp.max(jnp.where(live, scores, -jnp.inf), axis=-1), FLOOR_SCORE)
    hist_weights = jnp.where(live, jnp.exp(scores - hist_max[..., None]), 0.0)
    hist_total = jnp.sum(hist_weights, axis=-1)
    hist_numer = jnp.einsum(
        "mhtp,mphd->mthd",
        hist_weights.astype(jnp.bfloat16),
        vals_hist,
        preferred_element_type=jnp.float32,
    ).reshape(tok_rows, HEADS, HEAD)
    hist_max = jnp.transpose(hist_max, (0, 2, 1)).reshape(tok_rows, HEADS)
    hist_total = jnp.transpose(hist_total, (0, 2, 1)).reshape(tok_rows, HEADS)
    query_new = query_local.reshape(meet_count, new_count, heads_here, HEAD)
    key_new = key_local.reshape(meet_count, new_count, heads_here, HEAD)
    value_new = value_local.reshape(meet_count, new_count, heads_here, HEAD)
    new_scores = (
        jnp.einsum("mthd,mshd->mhts", query_new, key_new, preferred_element_type=jnp.float32)
        * scale
    )
    causal = (
        jnp.arange(new_count, dtype=jnp.int32)[:, None]
        >= jnp.arange(new_count, dtype=jnp.int32)[None, :]
    )[None, None]
    new_max = jnp.max(jnp.where(causal, new_scores, -jnp.inf), axis=-1)
    new_weights = jnp.where(causal, jnp.exp(new_scores - new_max[..., None]), 0.0)
    new_total = jnp.sum(new_weights, axis=-1)
    new_numer = jnp.einsum(
        "mhts,mshd->mthd",
        new_weights.astype(jnp.bfloat16),
        value_new,
        preferred_element_type=jnp.float32,
    ).reshape(tok_rows, heads_here, HEAD)
    new_max = jnp.transpose(new_max, (0, 2, 1)).reshape(tok_rows, heads_here)
    new_total = jnp.transpose(new_total, (0, 2, 1)).reshape(tok_rows, heads_here)
    own_part = (
        lax.dynamic_slice_in_dim(hist_max, head_start, heads_here, 1),
        lax.dynamic_slice_in_dim(hist_total, head_start, heads_here, 1),
        lax.dynamic_slice_in_dim(hist_numer, head_start, heads_here, 1),
    )
    joined_max, joined_total, joined_numer = combine_parts(
        own_part, (new_max, new_total, new_numer)
    )
    part_max = lax.dynamic_update_slice_in_dim(hist_max, joined_max, head_start, 1)
    part_total = lax.dynamic_update_slice_in_dim(hist_total, joined_total, head_start, 1)
    part_numer = lax.dynamic_update_slice_in_dim(hist_numer, joined_numer, head_start, 1)
    attended = finish_heads(
        (
            lax.all_to_all(
                part_max[None].astype(jnp.bfloat16), "ctx", split_axis=2, concat_axis=0, tiled=True
            ).astype(jnp.float32),
            lax.all_to_all(
                part_total[None].astype(jnp.bfloat16),
                "ctx",
                split_axis=2,
                concat_axis=0,
                tiled=True,
            ).astype(jnp.float32),
            lax.all_to_all(
                part_numer[None].astype(jnp.bfloat16),
                "ctx",
                split_axis=2,
                concat_axis=0,
                tiled=True,
            ).astype(jnp.float32),
        )
    )
    attended_flat = attended.reshape(tok_rows, cols_local)
    out_terms = jnp.dot(attended_flat, out_rows, preferred_element_type=jnp.float32)
    attn_out = lax.psum_scatter(
        out_terms.astype(jnp.bfloat16), "ctx", scatter_dimension=1, tiled=True
    )
    return (
        attn_out,
        key_local.reshape(tok_rows, cols_local),
        value_local.reshape(tok_rows, cols_local),
    )


def solution(mesh):
    return jax.shard_map(
        shards,
        mesh=mesh,
        in_specs=(
            P("wt", None),
            P("wt"),
            P(None, "ctx"),
            P("ctx"),
            P(),
            P("wt", None, "ctx"),
            P("ctx", "wt"),
            P("wt", "ctx", None),
            P("wt", "ctx", None),
            P("wt"),
        ),
        out_specs=(P("wt", "ctx"), P("wt", "ctx"), P("wt", "ctx")),
        check_vma=False,
    )
```

profile of v0, /device:TPU:0, one launch (start us, length us, event | category | flops | bytes accessed | tf_op | source)
XLA Modules:
  0.0 330.0 jit_solution(13239334160668740162)
XLA Ops:
  7.2 0.8 compare_select_fusion
  8.0 1.5 gather_fusion
  9.6 2.3 fusion.15
  12.0 0.7 all-gather.7.cloned.1.call-update
  12.9 0.8 multiply_cosine_fusion
  13.8 40.6 %all-gather.5.cloned.1.call-done = bf16[128,4096]{1,0:T(8,128)(2,1)} async-done(((bf16[128,512]{1,0:T(8,128)(2,1)}), bf16[128,4096]{1,0:T(8,128)(2,1)}) %all-gather.5.cloned.1.call-update) | async-done | bytes 1048592 | tf_op jit(solution)/shard_map/all_gather | solution.py:77
  54.3 1.5 fusion
  55.9 81.1 %all-gather.7.cloned.1.call-done = bf16[4096,3,512]{2,0,1:T(8,128)(2,1)} async-done(((bf16[1024,3,512]{2,0,1:T(8,128)(2,1)}), bf16[4096,3,512]{2,0,1:T(8,128)(2,1)}) %all-gather.7.cloned.1.call-update) | async-done | bytes 12582928 | tf_op jit(solution)/shard_map/all_gather | solution.py:83
  136.9 6.7 %fusion.18 = f32[128,3,512]{2,0,1:T(8,128)S(1)} fusion(bf16[4096,3,512]{2,0,1:T(8,128)(2,1)} %all-gather.7.cloned.1.call-done, bf16[128,4096]{1,0:T(8,128)(2,1)} %all-gather.5.cloned.1.call-done, f32[4096]{0:T(1024)S(1)} %copy-done.5, f32[128]{0:T(128)S(1)} %add_rsqrt_fusion), kind=kOutput, calls=%fused_computation.25 | convolution fusion | flops 1612709888 | bytes 14434816 | tf_op jit(solution)/shard_map/rd,dke->rke/dot_general | solution.py:86
  143.7 0.7 fusion.48
  144.5 1.1 copy.168
  145.6 0.9 subtract_convert_fusion
  146.5 0.6 copy-done.2
  147.1 0.7 pad_maximum_fusion
  147.8 0.8 copy.135
  148.6 0.5 all-gather.11.cloned.1.call-update
  149.3 0.9 concatenate.25
  150.2 0.9 concatenate.26
  151.3 0.8 concatenate.29
  152.0 0.7 slice.46
  153.1 1.7 copy.147
  154.8 1.2 select_reduce_fusion.1
  156.3 0.9 convert_element_type.110
  157.5 30.9 %all-gather.9.cloned.1.call-done = bf16[128,4096]{1,0:T(8,128)(2,1)} async-done(((bf16[128,512]{1,0:T(8,128)(2,1)}), bf16[128,4096]{1,0:T(8,128)(2,1)}) %all-gather.9.cloned.1.call-update) | async-done | bytes 1048592 | tf_op jit(solution)/shard_map/all_gather | solution.py:97
  188.3 1.5 copy.172
  189.8 2.9 select_reduce_fusion
  192.9 2.5 fusion.13
  196.2 0.7 reduce.3
  196.9 0.6 reshape.244
  197.5 3.5 %all-to-all-start.1 = ((bf16[8,2,256]{2,1,0:T(2,128)(2,1)}), bf16[8,2,256]{2,1,0:T(2,128)(2,1)S(1)}, u32[]{:S(2)}, u32[]{:S(2)}) async-start(bf16[8,2,256]{2,1,0:T(2,128)(2,1)} %reshape.244), calls=%async_computation.1 | async-start | bytes 16384 | tf_op jit(solution)/shard_map/all_to_all | solution.py:155
  201.0 4.3 %fusion.10 = f32[2,64,32,128]{3,1,2,0:T(8,128)} fusion(f32[2,32,64,128]{3,2,1,0:T(8,128)} %get-tuple-element.21, f32[2,32,64]{2,1,0:T(8,128)S(1)} %get-tuple-element.15, pred[2,128]{1,0:T(4,128)(4,1)S(1)} %broadcast_compare_fusion, bf16[2,128,4096]{2,1,0:T(8,128)(2,1)} %param.18), kind=kOutput, calls=%fused_computation.17 | convolution fusion | flops 136314880 | bytes 6308096 | tf_op jit(solution)/shard_map/mhtp,mphd->mthd/dot_general | solution.py:112
  205.4 0.7 reduce.2
  206.1 0.6 reshape.246
  206.9 2.8 copy.139
  209.8 1.3 copy-done.1
  211.1 1.3 copy.201
  212.4 6.0 %all-to-all-start.2 = ((bf16[8,2,256]{2,1,0:T(2,128)(2,1)}), bf16[8,2,256]{2,1,0:T(2,128)(2,1)S(1)}, u32[]{:S(2)}, u32[]{:S(2)}) async-start(bf16[8,2,256]{2,1,0:T(2,128)(2,1)} %reshape.246), calls=%async_computation.2 | async-start | bytes 16384 | tf_op jit(solution)/shard_map/all_to_all | solution.py:158
  218.4 2.1 bitcast_dynamic-update-slice_fusion
  220.6 1.8 convert_element_type.112
  222.4 1.4 copy.155
  223.8 1.1 all-to-all-done.2
  225.0 4.8 %all-to-all-start = ((bf16[1,128,32,128]{3,1,0,2:T(8,128)(2,1)}), bf16[1,128,32,128]{3,1,0,2:T(8,128)(2,1)}, u32[]{:S(2)}, u32[]{:S(2)}) async-start(bf16[1,128,32,128]{3,1,0,2:T(8,128)(2,1)} %copy.155), calls=%async_computation | async-start | bytes 2097152 | tf_op jit(solution)/shard_map/all_to_all | solution.py:165
  230.0 24.4 %all-to-all-done = bf16[1,128,32,128]{3,1,0,2:T(8,128)(2,1)} async-done(((bf16[1,128,32,128]{3,1,0,2:T(8,128)(2,1)}), bf16[1,128,32,128]{3,1,0,2:T(8,128)(2,1)}, u32[]{:S(2)}, u32[]{:S(2)}) %all-to-all-start) | async-done | bytes 1048608 | tf_op jit(solution)/shard_map/all_to_all | solution.py:165
  254.3 1.8 fusion.9
  256.4 4.0 %convolution_convert_fusion = bf16[128,4096]{1,0:T(8,128)(2,1)} fusion(bf16[128,512]{0,1:T(8,128)(2,1)S(1)} %bitcast.119, bf16[512,4096]{1,0:T(8,128)(2,1)} %all-gather.11.cloned.1.call-done), kind=kOutput, calls=%fused_computation.1 | convolution fusion | flops 537395200 | bytes 5373952 | tf_op jit(solution)/shard_map/dot_general | solution.py:175
  260.4 0.8 copy.166
  261.2 0.7 slice_bitcast_fusion
  261.9 61.7 %reduce-scatter.2.cloned.1.call-done = bf16[128,512]{1,0:T(8,128)(2,1)} async-done(((bf16[128,4096]{1,0:T(8,128)(2,1)}), bf16[128,512]{1,0:T(8,128)(2,1)}) %reduce-scatter.2.cloned.1.call-update) | async-done | bytes 131088 | tf_op jit(solution)/shard_map/reduce_scatter | solution.py:176
  (65 shorter events, 3.3 us)
Async XLA Ops:
  7.2 182.6 %copy-start = (bf16[2,128,4096]{2,1,0:T(8,128)(2,1)S(1)}, bf16[2,128,4096]{2,1,0:T(8,128)(2,1)}, u32[]{:S(2)}) copy-start(bf16[2,128,4096]{2,1,0:T(8,128)(2,1)} %param.17) | copy-start | bytes 6291460
  7.2 47.1 %all-gather.5.cloned.1.call-start = ((), (), s32[]{:S(2)}) async-start(), calls=%async_computation.4 | async-start | bytes 1179648 | tf_op jit(solution)/shard_map/all_gather | solution.py:77
  9.6 3.2 copy-start.6
  11.9 125.0 %copy-start.5 = (f32[4096]{0:T(1024)S(1)}, f32[4096]{0:T(1024)}, u32[]{:S(2)}) copy-start(f32[4096]{0:T(1024)} %param.14) | copy-start | bytes 49156
  11.9 125.0 %all-gather.7.cloned.1.call-start = ((), (), s32[]{:S(2)}) async-start(), calls=%async_computation.5 | async-start | bytes 15728640 | tf_op jit(solution)/shard_map/all_gather | solution.py:83
  12.7 175.6 %all-gather.9.cloned.1.call-start = ((), (), s32[]{:S(2)}) async-start(), calls=%async_computation.6 | async-start | bytes 1179648 | tf_op jit(solution)/shard_map/all_gather | solution.py:97
  146.5 0.6 copy-start.2
  146.5 1.3 copy-start.3
  148.6 107.8 %all-gather.11.cloned.1.call-start = ((), (), s32[]{:S(2)}) async-start(), calls=%async_computation.7 | async-start | bytes 5242880 | tf_op jit(solution)/shard_map/all_gather | solution.py:84
  197.5 14.9 %all-to-all-start.1 = ((bf16[8,2,256]{2,1,0:T(2,128)(2,1)}), bf16[8,2,256]{2,1,0:T(2,128)(2,1)S(1)}, u32[]{:S(2)}, u32[]{:S(2)}) async-start(bf16[8,2,256]{2,1,0:T(2,128)(2,1)} %reshape.244), calls=%async_computation.1 | async-start | bytes 16384 | tf_op jit(solution)/shard_map/all_to_all | solution.py:155
  209.7 1.3 copy-start.1
  212.4 12.6 %all-to-all-start.2 = ((bf16[8,2,256]{2,1,0:T(2,128)(2,1)}), bf16[8,2,256]{2,1,0:T(2,128)(2,1)S(1)}, u32[]{:S(2)}, u32[]{:S(2)}) async-start(bf16[8,2,256]{2,1,0:T(2,128)(2,1)} %reshape.246), calls=%async_computation.2 | async-start | bytes 16384 | tf_op jit(solution)/shard_map/all_to_all | solution.py:158
  225.0 29.4 %all-to-all-start = ((bf16[1,128,32,128]{3,1,0,2:T(8,128)(2,1)}), bf16[1,128,32,128]{3,1,0,2:T(8,128)(2,1)}, u32[]{:S(2)}, u32[]{:S(2)}) async-start(bf16[1,128,32,128]{3,1,0,2:T(8,128)(2,1)} %copy.155), calls=%async_computation | async-start | bytes 2097152 | tf_op jit(solution)/shard_map/all_to_all | solution.py:165
  229.8 93.7 %reduce-scatter.2.cloned.1.call-start = ((), (), s32[]{:S(2)}) async-start(), calls=%async_computation.8 | async-start | bytes 1179648 | tf_op jit(solution)/shard_map/reduce_scatter | solution.py:176
  256.4 4.0 %copy-start.4 = (bf16[128,4,128]{0,2,1:T(8,128)(2,1)S(1)}, bf16[128,4,128]{0,2,1:T(8,128)(2,1)}, u32[]{:S(2)}) copy-start(bf16[128,4,128]{0,2,1:T(8,128)(2,1)} %get-tuple-element.25) | copy-start | bytes 393220
Sparse Core Ops, SparseCore 0:
  12.1 42.2 all-gather.4
  55.9 80.9 all-gather.6
  148.7 39.5 all-gather.8
  189.7 33.3 all-gather.10
  260.5 62.9 reduce-scatter.1
where the time goes:
time: 331 us; the launch traced here: 330 us
  waiting for transfers between devices  241 us (73%)
  local copies, waits for them, and re-layouts  23.9 us (7%)
  matrix products  21.7 us (7%)
  other arithmetic  14.8 us (4%)
  starting transfers between devices  14.6 us (4%)
  between operations  14.1 us (4%)
    all_gather x1, waiting for transfers between devices, shards(): lax.all_gather(qkv_weight, 'wt', axis=0, tiled=True)  81.1 us
    reduce_scatter x1, waiting for transfers between devices, shards(): lax.psum_scatter(out_terms.astype(jnp.bfloat16), 'ctx', scatter_dimension...  61.7 us
    all_gather x1, waiting for transfers between devices, shards(): features = lax.all_gather(adapted, 'ctx', axis=1, tiled=True)  40.6 us
    all_gather x1, waiting for transfers between devices, shards(): lax.all_gather(query_local.reshape(tok_rows, cols_local), 'ctx', axis=1,...  30.9 us
    all_to_all x1, waiting for transfers between devices, shards(): lax.all_to_all(part_numer[None].astype(jnp.bfloat16), 'ctx', split_axis=2...  24.4 us
    dot_general x1, matrix products, shards(): jnp.einsum('rd,dke->rke', normed, qkv_full, preferred_element_type=jnp.fl...  6.75 us
  transfers between devices with their start and end apart: 8, of which 6 were waited for; matrix products, arithmetic and copies ran while one was open for 12% of the time, Pallas kernels for 0%

commit v1 on v0

v1 whole, which is shorter than its diff:
```python
import functools

import jax
import jax.numpy as jnp
from jax import lax
from jax.experimental import pallas as pl
from jax.experimental.pallas import tpu as pltpu
from jax.sharding import PartitionSpec as P

HEAD = 128
FLOOR_SCORE = -1e30
MESH = pl.DeviceIdType.MESH
LOW = 2


def layer_kernel(
    nc, nw, meets, hist,
    frames_ref, adapter_ref, bias_ref, gain_ref, cos_ref, sin_ref, live_ref,
    qkv_hbm, ow_hbm, k_hbm, v_hbm,
    out_ref, key_ref, value_ref,
    feat, xin, query_all, qkv_w, k_mem, v_mem, ow_all,
    proj_own, proj_send, pair_in, cross_send, cross_in,
    num_own, num_send, num_in, num_cross_send, num_cross_in,
    stat_own, stat_send, stat_in, stat_cross_send, stat_cross_in,
    sum_own, sum_send, sum_in, sum_cross_send, sum_cross_in,
    new_num, new_stat, attended,
    local_sem,
    fz_s, fz_r, fy_s, fy_r, fx_s, fx_r,
    pair_s, pair_r, cross_s, cross_r,
    qz_s, qz_r, qy_s, qy_r,
    ow_s, ow_r, owf_s, owf_r,
    ny_s, ny_r, nz_s, nz_r, ty_s, ty_r, tz_s, tz_r,
    by_s, by_r, bz_s, bz_r,
):
    nz, nx, ratio = nc // LOW, nw // 2, nc // nw
    rows, cols = key_ref.shape
    heads = cols // HEAD
    new = rows // meets
    c, w = lax.axis_index("ctx"), lax.axis_index("wt")
    z, y = lax.div(c, LOW), lax.rem(c, LOW)
    x, k = lax.div(w, 2), lax.rem(w, 2)
    other_y, other_k = 1 - y, 1 - k
    sibling_c = z * LOW + other_y
    sibling_w = x * 2 + other_k
    scale = HEAD ** (-0.5)
    pending = []

    def up(value, step, size):
        return lax.rem(value + step, size)

    def down(value, step, size):
        return lax.rem(value + size - step, size)

    def remote(src, dst, send, recv, to_c, to_w):
        return pltpu.make_async_remote_copy(
            src_ref=src, dst_ref=dst, send_sem=send, recv_sem=recv,
            device_id=(to_c, to_w), device_id_type=MESH,
        )

    def send(*parts):
        copy = remote(*parts)
        copy.start()
        pending.append(copy)

    def arrived(dst, send_sem, recv_sem):
        remote(dst, dst, send_sem, recv_sem, sibling_c, w).wait_recv()

    loads = [
        pltpu.make_async_copy(qkv_hbm, qkv_w, local_sem.at[0]),
        pltpu.make_async_copy(k_hbm, k_mem, local_sem.at[1]),
        pltpu.make_async_copy(v_hbm, v_mem, local_sem.at[2]),
        pltpu.make_async_copy(ow_hbm, ow_all.at[w], local_sem.at[3]),
    ]
    for load in loads:
        load.start()

    barrier = pltpu.get_barrier_semaphore()
    for step in range(1, nz):
        pl.semaphore_signal(
            barrier, inc=1, device_id=(up(z, step, nz) * LOW + y, w), device_id_type=MESH
        )
    pl.semaphore_signal(barrier, inc=1, device_id=(sibling_c, w), device_id_type=MESH)
    for step in range(1, nw):
        pl.semaphore_signal(barrier, inc=1, device_id=(c, up(w, step, nw)), device_id_type=MESH)
    adapted = jnp.dot(frames_ref[...], adapter_ref[...], preferred_element_type=jnp.float32)
    feat[c] = (adapted + bias_ref[...]).astype(jnp.bfloat16)
    pl.semaphore_wait(barrier, nz - 1 + 1 + nw - 1)

    def spread_z(buffer, s_sem, r_sem):
        for step in range(nz - 1, 0, -1):
            send(
                buffer.at[c], buffer.at[c], s_sem.at[step], r_sem.at[step],
                up(z, step, nz) * LOW + y, w,
            )

    def spread_y(buffer, block, step, s_sem, r_sem):
        send(buffer.at[block], buffer.at[block], s_sem.at[step], r_sem.at[step], sibling_c, w)

    def forward_copy(block):
        target = lax.div(block, ratio)
        slot = w * ratio + lax.rem(block, ratio)
        return target, slot, remote(
            feat.at[block], xin.at[slot], fx_s.at[block], fx_r.at[slot], c, target
        )

    def forward(block):
        target, slot, copy = forward_copy(block)

        @pl.when(target != w)
        def _():
            copy.start()

        @pl.when(target == w)
        def _():
            xin[slot] = feat[block]

    def z_block(step):
        return down(z, step, nz) * LOW + y

    def y_block(step):
        return down(z, step, nz) * LOW + other_y

    spread_y(feat, c, 0, fy_s, fy_r)
    spread_z(feat, fz_s, fz_r)
    forward(c)
    for step in range(nz):
        if step:
            arrived(feat.at[z_block(step)], fz_s.at[step], fz_r.at[step])
            spread_y(feat, z_block(step), step, fy_s, fy_r)
            forward(z_block(step))
        if step:
            arrived(feat.at[y_block(step - 1)], fy_s.at[step - 1], fy_r.at[step - 1])
            forward(y_block(step - 1))
    arrived(feat.at[y_block(nz - 1)], fy_s.at[nz - 1], fy_r.at[nz - 1])
    forward(y_block(nz - 1))

    loads[0].wait()

    def project(group):
        @pl.when(group != w)
        def _():
            for j in range(ratio):
                slot = group * ratio + j
                arrived(xin.at[slot], fx_s.at[j], fx_r.at[slot])

        scaled = [
            (xin[group * ratio + j].astype(jnp.float32) * gain_ref[w * ratio + j]).astype(
                jnp.bfloat16
            )
            for j in range(ratio)
        ]
        lhs = jnp.concatenate(scaled, axis=1)
        return [
            jnp.dot(lhs, qkv_w[kind], preferred_element_type=jnp.float32) for kind in range(3)
        ]

    @pl.loop(0, nx)
    def _(index):
        at = lax.rem(x + 1 + index, nx)
        terms = project(at * 2 + other_k)
        for kind in range(3):
            proj_send[at, kind] = terms[kind].astype(jnp.bfloat16)
        remote(
            proj_send.at[at], pair_in.at[at], pair_s.at[at], pair_r.at[at], c, sibling_w
        ).start()

    @pl.loop(0, nx)
    def _(index):
        at = lax.rem(x + 1 + index, nx)
        terms = project(at * 2 + k)
        for kind in range(3):
            proj_own[at, kind] = terms[kind]

    for step in range(1, nx):
        at = up(x, step, nx)
        arrived(pair_in.at[at], pair_s.at[at], pair_r.at[at])
        for kind in range(3):
            cross_send[step, kind] = (
                proj_own[at, kind] + pair_in[at, kind].astype(jnp.float32)
            ).astype(jnp.bfloat16)
        send(
            cross_send.at[step], cross_in.at[step], cross_s.at[step], cross_r.at[step],
            c, at * 2 + k,
        )

    squares = jnp.zeros((rows, 1), jnp.float32)
    for block in range(nc):
        wide = feat[block].astype(jnp.float32)
        squares += jnp.sum(wide * wide, axis=-1, keepdims=True)
    inverse = lax.rsqrt(squares / (nc * cols) + 1e-06)

    arrived(pair_in.at[x], pair_s.at[x], pair_r.at[x])
    for step in range(1, nx):
        arrived(cross_in.at[step], cross_s.at[step], cross_r.at[step])

    def projected(kind):
        total = proj_own[x, kind] + pair_in[x, kind].astype(jnp.float32)
        for step in range(1, nx):
            total += cross_in[step, kind].astype(jnp.float32)
        return total * inverse

    def rotated(values):
        pieces = []
        for head in range(heads):
            piece = values[:, head * HEAD : (head + 1) * HEAD]
            pieces.append(piece * cos_ref[...] + pltpu.roll(piece, HEAD // 2, 1) * sin_ref[...])
        return jnp.concatenate(pieces, axis=1).astype(jnp.bfloat16)

    query_all[c] = rotated(projected(0))
    spread_y(query_all, c, 0, qy_s, qy_r)
    spread_z(query_all, qz_s, qz_r)
    key_ref[...] = rotated(projected(1))
    value_ref[...] = projected(2).astype(jnp.bfloat16)

    loads[3].wait()
    send(ow_all.at[w], ow_all.at[w], ow_s.at[0], ow_r.at[0], c, sibling_w)
    for step in range(1, nx):
        send(
            ow_all.at[w], ow_all.at[w], ow_s.at[step], ow_r.at[step],
            c, up(x, step, nx) * 2 + k,
        )

    lanes = lax.broadcasted_iota(jnp.int32, (rows, HEAD), 1)

    def attend(query, keys, values, mask, meeting_mask):
        stat = jnp.zeros((rows, HEAD), jnp.float32)
        numers = []
        for head in range(heads):
            at = slice(head * HEAD, (head + 1) * HEAD)
            tops, totals, parts = [], [], []
            for m in range(meets):
                score = lax.dot_general(
                    query[m * new : (m + 1) * new, at], keys[m][:, at],
                    (((1,), (1,)), ((), ())), preferred_element_type=jnp.float32,
                ) * scale
                keep = mask[m] if meeting_mask else mask
                top = jnp.maximum(
                    jnp.max(jnp.where(keep, score, -jnp.inf), axis=-1, keepdims=True), FLOOR_SCORE
                )
                weight = jnp.where(keep, jnp.exp(score - top), 0.0)
                tops.append(top)
                totals.append(jnp.sum(weight, axis=-1, keepdims=True))
                parts.append(
                    jnp.dot(
                        weight.astype(jnp.bfloat16), values[m][:, at],
                        preferred_element_type=jnp.float32,
                    )
                )
            stat = jnp.where(lanes == head, jnp.concatenate(tops, axis=0), stat)
            stat = jnp.where(lanes == heads + head, jnp.concatenate(totals, axis=0), stat)
            numers.append(jnp.concatenate(parts, axis=0))
        return jnp.concatenate(numers, axis=1), stat

    causal = lax.broadcasted_iota(jnp.int32, (new, new), 0) >= lax.broadcasted_iota(
        jnp.int32, (new, new), 1
    )
    new_keys, new_values = key_ref[...], value_ref[...]
    numer, stat = attend(
        query_all[c],
        [new_keys[m * new : (m + 1) * new] for m in range(meets)],
        [new_values[m * new : (m + 1) * new] for m in range(meets)],
        causal, False,
    )
    new_num[...] = numer
    new_stat[...] = stat

    loads[1].wait()
    loads[2].wait()

    def history(block):
        at = pl.ds(pl.multiple_of(block * cols, cols), cols)
        return attend(
            query_all[block],
            [k_mem[m, :, at] for m in range(meets)],
            [v_mem[m, :, at] for m in range(meets)],
            [jnp.broadcast_to(live_ref[m] > 0.5, (new, hist)) for m in range(meets)], True,
        )

    def packed(stat):
        return jnp.transpose(stat)[: stat_send.shape[1]]

    def unpacked(short):
        filled = jnp.concatenate(
            [short, jnp.zeros((HEAD - short.shape[0], rows), jnp.float32)], axis=0
        )
        return jnp.transpose(filled)

    def merge(left, right):
        left_num, left_stat = left
        right_num, right_stat = right
        joint = jnp.maximum(left_stat, right_stat)
        left_scale = jnp.exp(left_stat - joint)
        right_scale = jnp.exp(right_stat - joint)
        stat = jnp.where(lanes < heads, joint, 0.0)
        pieces = []
        for head in range(heads):
            at = slice(head * HEAD, (head + 1) * HEAD)
            one, two = left_scale[:, head : head + 1], right_scale[:, head : head + 1]
            pieces.append(left_num[:, at] * one + right_num[:, at] * two)
            total = (
                left_stat[:, heads + head : heads + head + 1] * one
                + right_stat[:, heads + head : heads + head + 1] * two
            )
            stat = jnp.where(lanes == heads + head, total, stat)
        return jnp.concatenate(pieces, axis=1), stat

    for step in range(1, nz):
        arrived(query_all.at[z_block(step)], qz_s.at[step], qz_r.at[step])
        spread_y(query_all, z_block(step), step, qy_s, qy_r)

    @pl.loop(0, nz)
    def _(step):
        block = y_block(step)
        arrived(query_all.at[block], qy_s.at[step], qy_r.at[step])
        numer, stat = history(block)
        num_send[step] = numer.astype(jnp.bfloat16)
        stat_send[step] = packed(stat)
        remote(
            num_send.at[step], num_in.at[step], ny_s.at[step], ny_r.at[step], sibling_c, w
        ).start()
        remote(
            stat_send.at[step], stat_in.at[step], ty_s.at[step], ty_r.at[step], sibling_c, w
        ).start()

    @pl.loop(0, nz)
    def _(index):
        step = lax.rem(index + 1, nz)
        block = z_block(step)
        own = history(block)
        arrived(num_in.at[step], ny_s.at[step], ny_r.at[step])
        arrived(stat_in.at[step], ty_s.at[step], ty_r.at[step])
        numer, stat = merge(
            own, (num_in[step].astype(jnp.float32), unpacked(stat_in[step]))
        )

        @pl.when(step > 0)
        def _():
            num_cross_send[step] = numer.astype(jnp.bfloat16)
            stat_cross_send[step] = packed(stat)
            remote(
                num_cross_send.at[step], num_cross_in.at[step], nz_s.at[step], nz_r.at[step],
                block, w,
            ).start()
            remote(
                stat_cross_send.at[step], stat_cross_in.at[step], tz_s.at[step], tz_r.at[step],
                block, w,
            ).start()

        @pl.when(step == 0)
        def _():
            numer_all, stat_all = merge((numer, stat), (new_num[...], new_stat[...]))
            num_own[...] = numer_all
            stat_own[...] = stat_all

    for step in range(1, nx):
        origin = down(x, step, nx) * 2 + k
        arrived(ow_all.at[origin], ow_s.at[step], ow_r.at[step])
        send(
            ow_all.at[origin], ow_all.at[origin], owf_s.at[step], owf_r.at[step], c, sibling_w
        )

    for step in range(1, nz):
        arrived(num_cross_in.at[step], nz_s.at[step], nz_r.at[step])
        arrived(stat_cross_in.at[step], tz_s.at[step], tz_r.at[step])
        numer, stat = merge(
            (num_own[...], stat_own[...]),
            (num_cross_in[step].astype(jnp.float32), unpacked(stat_cross_in[step])),
        )
        num_own[...] = numer
        stat_own[...] = stat
    stat = stat_own[...]
    for head in range(heads):
        at = slice(head * HEAD, (head + 1) * HEAD)
        attended[:, at] = (
            num_own[:, at] / stat[:, heads + head : heads + head + 1]
        ).astype(jnp.bfloat16)

    arrived(ow_all.at[sibling_w], ow_s.at[0], ow_r.at[0])
    for step in range(1, nx):
        origin = down(x, step, nx) * 2 + other_k
        arrived(ow_all.at[origin], owf_s.at[step], owf_r.at[step])

    def out_term(block):
        at = pl.ds(pl.multiple_of(lax.rem(block, ratio) * cols, cols), cols)
        return jnp.dot(
            attended[...], ow_all[lax.div(block, ratio), :, at],
            preferred_element_type=jnp.float32,
        )

    @pl.loop(0, nz)
    def _(index):
        step = lax.rem(index + 1, nz)
        sum_send[step] = out_term(y_block(step)).astype(jnp.bfloat16)
        remote(
            sum_send.at[step], sum_in.at[step], by_s.at[step], by_r.at[step], sibling_c, w
        ).start()

    @pl.loop(0, nz)
    def _(index):
        step = lax.rem(index + 1, nz)
        block = z_block(step)
        term = out_term(block)
        arrived(sum_in.at[step], by_s.at[step], by_r.at[step])
        term += sum_in[step].astype(jnp.float32)

        @pl.when(step > 0)
        def _():
            sum_cross_send[step] = term.astype(jnp.bfloat16)
            remote(
                sum_cross_send.at[step], sum_cross_in.at[step], bz_s.at[step], bz_r.at[step],
                block, w,
            ).start()

        @pl.when(step == 0)
        def _():
            sum_own[...] = term

    total = sum_own[...]
    for step in range(1, nz):
        arrived(sum_cross_in.at[step], bz_s.at[step], bz_r.at[step])
        total += sum_cross_in[step].astype(jnp.float32)
    out_ref[...] = total.astype(jnp.bfloat16)

    def left(src, send_sem, recv_sem):
        remote(src, src, send_sem, recv_sem, sibling_c, w).wait_send()

    for copy in pending:
        copy.wait_send()
    for block in range(nc):
        target, _, copy = forward_copy(block)

        @pl.when(target != w)
        def _():
            copy.wait_send()

    for at in range(nx):
        left(proj_send.at[at], pair_s.at[at], pair_r.at[at])
    for step in range(nz):
        left(num_send.at[step], ny_s.at[step], ny_r.at[step])
        left(stat_send.at[step], ty_s.at[step], ty_r.at[step])
        left(sum_send.at[step], by_s.at[step], by_r.at[step])
        if step:
            left(num_cross_send.at[step], nz_s.at[step], nz_r.at[step])
            left(stat_cross_send.at[step], tz_s.at[step], tz_r.at[step])
            left(sum_cross_send.at[step], bz_s.at[step], bz_r.at[step])


def shards(
    nc, nw,
    frames, span_source, adapter_weight, adapter_bias, norm_gain,
    qkv_weight, out_weight, k_cache, v_cache, lengths,
):
    rows, audio_width = frames.shape
    group_spans = span_source.shape[0]
    meets, hist, width = k_cache.shape
    depth, _, cols = qkv_weight.shape
    new = rows // meets
    nz, nx = nc // LOW, nw // 2
    heads = cols // HEAD
    short = max(8, (2 * heads + 7) // 8 * 8)
    ordered = frames.reshape(group_spans, rows // group_spans, audio_width)[span_source].reshape(
        rows, audio_width
    )
    half = HEAD // 2
    positions = (lengths[:, None] + jnp.arange(new, dtype=jnp.int32)[None, :]).reshape(rows)
    freq = 10000.0 ** (-2.0 * jnp.arange(half, dtype=jnp.float32) / HEAD)
    angle = positions.astype(jnp.float32)[:, None] * freq[None, :]
    cosine, sine = jnp.cos(angle), jnp.sin(angle)
    cosines = jnp.concatenate([cosine, cosine], axis=1)
    sines = jnp.concatenate([-sine, sine], axis=1)
    place = lax.axis_index("ctx") * hist + jnp.arange(hist, dtype=jnp.int32)
    live = (place[None, :] < lengths[:, None]).astype(jnp.float32)[:, None, :]
    vmem = pl.BlockSpec(memory_space=pltpu.VMEM)
    anywhere = pl.BlockSpec(memory_space=pl.ANY)
    half_type, full_type = jnp.bfloat16, jnp.float32
    block = (rows, cols)
    dma = lambda count: pltpu.SemaphoreType.DMA((count,))
    result = jax.ShapeDtypeStruct(block, half_type)
    return pl.pallas_call(
        functools.partial(layer_kernel, nc, nw, meets, hist),
        out_shape=(result, result, result),
        in_specs=[vmem] * 7 + [anywhere] * 4,
        out_specs=(vmem, vmem, vmem),
        scratch_shapes=[
            pltpu.VMEM((nc,) + block, half_type),
            pltpu.VMEM((nc,) + block, half_type),
            pltpu.VMEM((nc,) + block, half_type),
            pltpu.VMEM((3, depth, cols), half_type),
            pltpu.VMEM((meets, hist, width), half_type),
            pltpu.VMEM((meets, hist, width), half_type),
            pltpu.VMEM((nw,) + out_weight.shape, half_type),
            pltpu.VMEM((nx, 3) + block, full_type),
            pltpu.VMEM((nx, 3) + block, half_type),
            pltpu.VMEM((nx, 3) + block, half_type),
            pltpu.VMEM((nx, 3) + block, half_type),
            pltpu.VMEM((nx, 3) + block, half_type),
            pltpu.VMEM(block, full_type),
            pltpu.VMEM((nz,) + block, half_type),
            pltpu.VMEM((nz,) + block, half_type),
            pltpu.VMEM((nz,) + block, half_type),
            pltpu.VMEM((nz,) + block, half_type),
            pltpu.VMEM((rows, HEAD), full_type),
            pltpu.VMEM((nz, short, rows), full_type),
            pltpu.VMEM((nz, short, rows), full_type),
            pltpu.VMEM((nz, short, rows), full_type),
            pltpu.VMEM((nz, short, rows), full_type),
            pltpu.VMEM(block, full_type),
            pltpu.VMEM((nz,) + block, half_type),
            pltpu.VMEM((nz,) + block, half_type),
            pltpu.VMEM((nz,) + block, half_type),
            pltpu.VMEM((nz,) + block, half_type),
            pltpu.VMEM(block, full_type),
            pltpu.VMEM((rows, HEAD), full_type),
            pltpu.VMEM(block, half_type),
            dma(4),
            dma(nz), dma(nz), dma(nz), dma(nz), dma(nc), dma(nc),
            dma(nx), dma(nx), dma(nx), dma(nx),
            dma(nz), dma(nz), dma(nz), dma(nz),
            dma(nx), dma(nx), dma(nx), dma(nx),
            dma(nz), dma(nz), dma(nz), dma(nz), dma(nz), dma(nz), dma(nz), dma(nz),
            dma(nz), dma(nz), dma(nz), dma(nz),
        ],
        compiler_params=pltpu.CompilerParams(
            collective_id=0, has_side_effects=True, vmem_limit_bytes=48 * 1024 * 1024
        ),
        cost_estimate=pl.CostEstimate(
            flops=8 * rows * depth * 3 * cols,
            bytes_accessed=2 * (3 * depth * cols + 2 * meets * hist * width),
            transcendentals=0,
        ),
    )(
        ordered, adapter_weight, adapter_bias.reshape(1, cols), norm_gain.reshape(nc, 1, cols),
        cosines, sines, live,
        jnp.transpose(qkv_weight, (1, 0, 2)), out_weight, k_cache, v_cache,
    )


def solution(mesh):
    nc, nw = mesh.shape["ctx"], mesh.shape["wt"]
    return jax.shard_map(
        functools.partial(shards, nc, nw),
        mesh=mesh,
        in_specs=(
            P("wt", None),
            P("wt"),
            P(None, "ctx"),
            P("ctx"),
            P(),
            P("wt", None, "ctx"),
            P("ctx", "wt"),
            P("wt", "ctx", None),
            P("wt", "ctx", None),
            P("wt"),
        ),
        out_specs=(P("wt", "ctx"), P("wt", "ctx"), P("wt", "ctx")),
        check_vma=False,
    )
```

time: 331 us -> 114 us (0.34)
  waiting for transfers between devices: 241 us -> 0 us
  Pallas kernels: 0 us -> 101 us
  matrix products: 21.7 us -> 0 us
  local copies, waits for them, and re-layouts: 23.9 us -> 9.1 us
  starting transfers between devices: 14.6 us -> 0 us
  between operations: 14.1 us -> 0.7 us
  other arithmetic: 14.8 us -> 2.54 us
    all_gather x4 -> x0, waiting for transfers between devices: 152 us -> none  [the longest x1 81.1 us: shards(): lax.all_gather(qkv_weight, 'wt', axis=0, tiled=True)]
    pallas_call x0 -> x1, Pallas kernels: none -> 101 us  [shards(): pl.pallas_call(functools.partial(layer_kernel, nc, nw, meets, hist), out_...]
    reduce_scatter x1 -> x0, waiting for transfers between devices: 61.7 us -> none  [shards(): lax.psum_scatter(out_terms.astype(jnp.bfloat16), 'ctx', scatter_dimension...]
    all_to_all x3 -> x0, waiting for transfers between devices: 25.5 us -> none  [the longest x1 24.4 us: shards(): lax.all_to_all(part_numer[None].astype(jnp.bfloat16), 'ctx', split_axis=2...]
    dot_general x7 -> x0, matrix products: 21.7 us -> none  [the longest x1 6.75 us: shards(): jnp.einsum('rd,dke->rke', normed, qkv_full, preferred_element_type=jnp.fl...]
    all_to_all x3 -> x0, starting transfers between devices: 14.4 us -> none  [the longest x1 6.04 us: shards(): lax.all_to_all(part_total[None].astype(jnp.bfloat16), 'ctx', split_axis=2...]
    reduce_sum x5 -> x0, other arithmetic: 5.92 us -> none  [the longest x1 2.54 us: shards(): hist_total = jnp.sum(hist_weights, axis=-1)]
    concatenate x8 -> x0, local copies, waits for them, and re-layouts: 4.82 us -> none  [rotate(): jnp.concatenate([first * cosine - second * sine, second * cosine + first...]
  transfers between devices with their start and end apart: 8 -> 0, of which waited for: 6 -> 0; matrix products, arithmetic and copies ran while one was open for 12% -> 0% of each run, Pallas kernels for 0% -> 0%
where the time goes in v1:
time: 114 us; the launch traced here: 113 us
  Pallas kernels  101 us (89%)
  local copies, waits for them, and re-layouts  9.1 us (8%)
  other arithmetic  2.54 us (2%)
    pallas_call x1, Pallas kernels, shards(): pl.pallas_call(functools.partial(layer_kernel, nc, nw, meets, hist), out_...  101 us
    unnamed x15, local copies, waits for them, and re-layouts  8.45 us

profile of v1, /device:TPU:0, one launch (start us, length us, event | category | flops | bytes accessed | tf_op | source)
XLA Modules:
  0.0 113.3 jit_solution(17736331608818792869)
XLA Ops:
  0.6 0.0 copy-start
  0.7 0.9 copy-done
  1.6 0.7 compare_select_fusion
  2.3 0.7 compare_convert_fusion.live_ref
  3.0 0.7 add_convert_fusion
  3.7 0.1 convert_element_type.21
  3.8 0.3 fusion
  4.1 0.1 pad_maximum_fusion
  4.2 0.6 gather_fusion
  4.8 0.0 copy-start.1
  4.8 1.6 %copy-done.1 = bf16[2,128,4096]{2,1,0:T(8,128)(2,1)S(1)} copy-done((bf16[2,128,4096]{2,1,0:T(8,128)(2,1)S(1)}, bf16[2,128,4096]{2,1,0:T(8,128)(2,1)}, u32[]{:S(2)}) %copy-start.1) | copy-done | bytes 2097176
  6.4 0.0 copy-start.2
  6.4 1.3 %copy-done.2 = bf16[1280,512]{1,0:T(8,128)(2,1)S(1)} copy-done((bf16[1280,512]{1,0:T(8,128)(2,1)S(1)}, bf16[1280,512]{1,0:T(8,128)(2,1)}, u32[]{:S(2)}) %copy-start.2) | copy-done | bytes 1310744
  7.7 0.0 copy-start.3
  7.7 1.2 %copy-done.3 = bf16[512,1024]{1,0:T(8,128)(2,1)S(1)} copy-done((bf16[512,1024]{1,0:T(8,128)(2,1)S(1)}, bf16[512,1024]{1,0:T(8,128)(2,1)}, u32[]{:S(2)}) %copy-start.3) | copy-done | bytes 1048600
  9.0 0.0 copy-start.4
  9.0 0.7 copy-done.4
  9.7 0.0 copy-start.5
  9.7 0.7 copy-done.5
  10.4 101.0 %shard_map.121 = (bf16[128,512]{1,0:T(8,128)(2,1)S(1)}, bf16[128,512]{1,0:T(8,128)(2,1)S(1)}, bf16[128,512]{1,0:T(8,128)(2,1)S(1)}) custom-call(bf16[128,1280]{1,0:T(8,128)(2,1)S(1)} %bitcast.6, bf16[1280,512]{1,0:T(8,128)(2,1)S(1)} %copy-done.2, f32[1,512]{1,0:T(1,128)S(1)} %bitcast.8, f32[8,1,512]{2,1,0:T(1,128)S(1)} %bitcast.7, ...), custom_call_target="tpu_custom_call" | custom-call | flops 1610612736 | bytes 7340032 | tf_op jit(solution)/shard_map/pallas_call | solution.py:479
  111.3 0.7 copy.16
  112.0 0.7 copy.17
  112.7 0.7 copy.18
  (3 shorter events, 0.0 us)
Async XLA Ops:
  0.6 1.0 copy-start
  4.8 1.6 %copy-start.1 = (bf16[2,128,4096]{2,1,0:T(8,128)(2,1)S(1)}, bf16[2,128,4096]{2,1,0:T(8,128)(2,1)}, u32[]{:S(2)}) copy-start(bf16[2,128,4096]{2,1,0:T(8,128)(2,1)} %k_hbm.1) | copy-start | bytes 6291460
  6.4 1.3 %copy-start.2 = (bf16[1280,512]{1,0:T(8,128)(2,1)S(1)}, bf16[1280,512]{1,0:T(8,128)(2,1)}, u32[]{:S(2)}) copy-start(bf16[1280,512]{1,0:T(8,128)(2,1)} %adapter_ref.1) | copy-start | bytes 3932164
  7.7 1.2 %copy-start.3 = (bf16[512,1024]{1,0:T(8,128)(2,1)S(1)}, bf16[512,1024]{1,0:T(8,128)(2,1)}, u32[]{:S(2)}) copy-start(bf16[512,1024]{1,0:T(8,128)(2,1)} %ow_hbm.1) | copy-start | bytes 3145732
  9.0 0.7 copy-start.4
  9.7 0.7 copy-start.5

commit v2 on v1

--- a/solution.py
+++ b/solution.py
@@ -1,4 +1,5 @@
 import functools
+import math
 
 import jax
 import jax.numpy as jnp
@@ -15,9 +16,10 @@
 
 def layer_kernel(
     nc, nw, meets, hist,
-    frames_ref, adapter_ref, bias_ref, gain_ref, cos_ref, sin_ref, live_ref,
-    qkv_hbm, ow_hbm, k_hbm, v_hbm,
+    source_ref, lengths_ref,
+    frames_hbm, adapter_hbm, bias_hbm, gain_hbm, qkv_hbm, ow_hbm, k_hbm, v_hbm,
     out_ref, key_ref, value_ref,
+    frames_ref, adapter_ref, bias_ref, gain_ref, cos_ref, sin_ref, lhs,
     feat, xin, query_all, qkv_w, k_mem, v_mem, ow_all,
     proj_own, proj_send, pair_in, cross_send, cross_in,
     num_own, num_send, num_in, num_cross_send, num_cross_in,
@@ -70,8 +72,12 @@
         pltpu.make_async_copy(k_hbm, k_mem, local_sem.at[1]),
         pltpu.make_async_copy(v_hbm, v_mem, local_sem.at[2]),
         pltpu.make_async_copy(ow_hbm, ow_all.at[w], local_sem.at[3]),
+        pltpu.make_async_copy(frames_hbm, frames_ref, local_sem.at[4]),
+        pltpu.make_async_copy(adapter_hbm, adapter_ref, local_sem.at[5]),
+        pltpu.make_async_copy(bias_hbm, bias_ref, local_sem.at[6]),
+        pltpu.make_async_copy(gain_hbm, gain_ref, local_sem.at[7]),
     ]
-    for load in loads:
+    for load in loads[4:] + loads[:4]:
         load.start()
 
     barrier = pltpu.get_barrier_semaphore()
@@ -82,7 +88,11 @@
     pl.semaphore_signal(barrier, inc=1, device_id=(sibling_c, w), device_id_type=MESH)
     for step in range(1, nw):
         pl.semaphore_signal(barrier, inc=1, device_id=(c, up(w, step, nw)), device_id_type=MESH)
-    adapted = jnp.dot(frames_ref[...], adapter_ref[...], preferred_element_type=jnp.float32)
+    for load in loads[4:]:
+        load.wait()
+    spans = frames_ref.shape[0]
+    ordered = jnp.concatenate([frames_ref[source_ref[slot]] for slot in range(spans)], axis=0)
+    adapted = jnp.dot(ordered, adapter_ref[...], preferred_element_type=jnp.float32)
     feat[c] = (adapted + bias_ref[...]).astype(jnp.bfloat16)
     pl.semaphore_wait(barrier, nz - 1 + 1 + nw - 1)
 
@@ -120,9 +130,21 @@
     def y_block(step):
         return down(z, step, nz) * LOW + other_y
 
+    lanes = lax.broadcasted_iota(jnp.int32, (rows, HEAD), 1)
+    tokens = lax.broadcasted_iota(jnp.int32, (rows, HEAD), 0)
+
     spread_y(feat, c, 0, fy_s, fy_r)
     spread_z(feat, fz_s, fz_r)
     forward(c)
+
+    place = tokens + lengths_ref[0]
+    for m in range(1, meets):
+        place = jnp.where(tokens >= m * new, tokens - m * new + lengths_ref[m], place)
+    twice = jnp.where(lanes < HEAD // 2, lanes, lanes - HEAD // 2).astype(jnp.float32)
+    angle = place.astype(jnp.float32) * jnp.exp(twice * (-2.0 / HEAD * math.log(10000.0)))
+    cos_ref[...] = jnp.cos(angle)
+    sin_ref[...] = jnp.sin(angle) * jnp.where(lanes < HEAD // 2, -1.0, 1.0)
+
     for step in range(nz):
         if step:
             arrived(feat.at[z_block(step)], fz_s.at[step], fz_r.at[step])
@@ -136,52 +158,59 @@
 
     loads[0].wait()
 
-    def project(group):
-        @pl.when(group != w)
-        def _():
+    def gather_rows(side, core):
+        for index in range(nx):
+            group = index * 2 + core
+
+            @pl.when(group != w)
+            def _():
+                for j in range(ratio):
+                    slot = group * ratio + j
+                    arrived(xin.at[slot], fx_s.at[j], fx_r.at[slot])
+
             for j in range(ratio):
-                slot = group * ratio + j
-                arrived(xin.at[slot], fx_s.at[j], fx_r.at[slot])
-
-        scaled = [
-            (xin[group * ratio + j].astype(jnp.float32) * gain_ref[w * ratio + j]).astype(
-                jnp.bfloat16
+                lhs[side, pl.ds(index * rows, rows), pl.ds(j * cols, cols)] = (
+                    xin[group * ratio + j].astype(jnp.float32) * gain_ref[w * ratio + j]
+                ).astype(jnp.bfloat16)
+
+    def project(side, kind):
+        total = jnp.dot(lhs[side], qkv_w[kind], preferred_element_type=jnp.float32)
+        return [total[at * rows : (at + 1) * rows] for at in range(nx)]
+
+    def project_pair(kind):
+        for at, term in enumerate(project(1, kind)):
+            proj_send[at, kind] = term.astype(jnp.bfloat16)
+            send(
+                proj_send.at[at, kind], pair_in.at[at, kind],
+                pair_s.at[at * 3 + kind], pair_r.at[at * 3 + kind], c, sibling_w,
             )
-            for j in range(ratio)
-        ]
-        lhs = jnp.concatenate(scaled, axis=1)
-        return [
-            jnp.dot(lhs, qkv_w[kind], preferred_element_type=jnp.float32) for kind in range(3)
-        ]
-
-    @pl.loop(0, nx)
-    def _(index):
-        at = lax.rem(x + 1 + index, nx)
-        terms = project(at * 2 + other_k)
-        for kind in range(3):
-            proj_send[at, kind] = terms[kind].astype(jnp.bfloat16)
-        remote(
-            proj_send.at[at], pair_in.at[at], pair_s.at[at], pair_r.at[at], c, sibling_w
-        ).start()
-
-    @pl.loop(0, nx)
-    def _(index):
-        at = lax.rem(x + 1 + index, nx)
-        terms = project(at * 2 + k)
-        for kind in range(3):
-            proj_own[at, kind] = terms[kind]
-
-    for step in range(1, nx):
-        at = up(x, step, nx)
-        arrived(pair_in.at[at], pair_s.at[at], pair_r.at[at])
-        for kind in range(3):
+
+    def project_own(kind):
+        for at, term in enumerate(project(0, kind)):
+            proj_own[at, kind] = term
+
+    def pass_on(kind):
+        for at in range(nx):
+            arrived(
+                pair_in.at[at, kind], pair_s.at[at * 3 + kind], pair_r.at[at * 3 + kind]
+            )
+        for step in range(1, nx):
+            at = up(x, step, nx)
             cross_send[step, kind] = (
                 proj_own[at, kind] + pair_in[at, kind].astype(jnp.float32)
             ).astype(jnp.bfloat16)
-        send(
-            cross_send.at[step], cross_in.at[step], cross_s.at[step], cross_r.at[step],
-            c, at * 2 + k,
-        )
+            send(
+                cross_send.at[step, kind], cross_in.at[step, kind],
+                cross_s.at[step * 3 + kind], cross_r.at[step * 3 + kind], c, at * 2 + k,
+            )
+
+    gather_rows(1, other_k)
+    project_pair(0)
+    gather_rows(0, k)
+    project_own(0)
+    pass_on(0)
+    project_pair(1)
+    project_pair(2)
 
     squares = jnp.zeros((rows, 1), jnp.float32)
     for block in range(nc):
@@ -189,13 +218,12 @@
         squares += jnp.sum(wide * wide, axis=-1, keepdims=True)
     inverse = lax.rsqrt(squares / (nc * cols) + 1e-06)
 
-    arrived(pair_in.at[x], pair_s.at[x], pair_r.at[x])
-    for step in range(1, nx):
-        arrived(cross_in.at[step], cross_s.at[step], cross_r.at[step])
-
     def projected(kind):
         total = proj_own[x, kind] + pair_in[x, kind].astype(jnp.float32)
         for step in range(1, nx):
+            arrived(
+                cross_in.at[step, kind], cross_s.at[step * 3 + kind], cross_r.at[step * 3 + kind]
+            )
             total += cross_in[step, kind].astype(jnp.float32)
         return total * inverse
 
@@ -209,8 +237,9 @@
     query_all[c] = rotated(projected(0))
     spread_y(query_all, c, 0, qy_s, qy_r)
     spread_z(query_all, qz_s, qz_r)
-    key_ref[...] = rotated(projected(1))
-    value_ref[...] = projected(2).astype(jnp.bfloat16)
+    for kind in (1, 2):
+        project_own(kind)
+        pass_on(kind)
 
     loads[3].wait()
     send(ow_all.at[w], ow_all.at[w], ow_s.at[0], ow_r.at[0], c, sibling_w)
@@ -220,7 +249,11 @@
             c, up(x, step, nx) * 2 + k,
         )
 
-    lanes = lax.broadcasted_iota(jnp.int32, (rows, HEAD), 1)
+    for step in range(1, nz):
+        arrived(query_all.at[z_block(step)], qz_s.at[step], qz_r.at[step])
+        spread_y(query_all, z_block(step), step, qy_s, qy_r)
+    key_ref[...] = rotated(projected(1))
+    value_ref[...] = projected(2).astype(jnp.bfloat16)
 
     def attend(query, keys, values, mask, meeting_mask):
         stat = jnp.zeros((rows, HEAD), jnp.float32)
@@ -267,13 +300,15 @@
     loads[1].wait()
     loads[2].wait()
 
+    cached = c * hist + lax.broadcasted_iota(jnp.int32, (new, hist), 1)
+
     def history(block):
         at = pl.ds(pl.multiple_of(block * cols, cols), cols)
         return attend(
             query_all[block],
             [k_mem[m, :, at] for m in range(meets)],
             [v_mem[m, :, at] for m in range(meets)],
-            [jnp.broadcast_to(live_ref[m] > 0.5, (new, hist)) for m in range(meets)], True,
+            [cached < lengths_ref[m] for m in range(meets)], True,
         )
 
     def packed(stat):
@@ -304,10 +339,6 @@
             stat = jnp.where(lanes == heads + head, total, stat)
         return jnp.concatenate(pieces, axis=1), stat
 
-    for step in range(1, nz):
-        arrived(query_all.at[z_block(step)], qz_s.at[step], qz_r.at[step])
-        spread_y(query_all, z_block(step), step, qy_s, qy_r)
-
     @pl.loop(0, nz)
     def _(step):
         block = y_block(step)
@@ -433,8 +464,6 @@
         def _():
             copy.wait_send()
 
-    for at in range(nx):
-        left(proj_send.at[at], pair_s.at[at], pair_r.at[at])
     for step in range(nz):
         left(num_send.at[step], ny_s.at[step], ny_r.at[step])
         left(stat_send.at[step], ty_s.at[step], ty_r.at[step])
@@ -454,23 +483,11 @@
     group_spans = span_source.shape[0]
     meets, hist, width = k_cache.shape
     depth, _, cols = qkv_weight.shape
-    new = rows // meets
     nz, nx = nc // LOW, nw // 2
     heads = cols // HEAD
     short = max(8, (2 * heads + 7) // 8 * 8)
-    ordered = frames.reshape(group_spans, rows // group_spans, audio_width)[span_source].reshape(
-        rows, audio_width
-    )
-    half = HEAD // 2
-    positions = (lengths[:, None] + jnp.arange(new, dtype=jnp.int32)[None, :]).reshape(rows)
-    freq = 10000.0 ** (-2.0 * jnp.arange(half, dtype=jnp.float32) / HEAD)
-    angle = positions.astype(jnp.float32)[:, None] * freq[None, :]
-    cosine, sine = jnp.cos(angle), jnp.sin(angle)
-    cosines = jnp.concatenate([cosine, cosine], axis=1)
-    sines = jnp.concatenate([-sine, sine], axis=1)
-    place = lax.axis_index("ctx") * hist + jnp.arange(hist, dtype=jnp.int32)
-    live = (place[None, :] < lengths[:, None]).astype(jnp.float32)[:, None, :]
     vmem = pl.BlockSpec(memory_space=pltpu.VMEM)
+    smem = pl.BlockSpec(memory_space=pltpu.SMEM)
     anywhere = pl.BlockSpec(memory_space=pl.ANY)
     half_type, full_type = jnp.bfloat16, jnp.float32
     block = (rows, cols)
@@ -479,9 +496,16 @@
     return pl.pallas_call(
         functools.partial(layer_kernel, nc, nw, meets, hist),
         out_shape=(result, result, result),
-        in_specs=[vmem] * 7 + [anywhere] * 4,
+        in_specs=[smem] * 2 + [anywhere] * 8,
         out_specs=(vmem, vmem, vmem),
         scratch_shapes=[
+            pltpu.VMEM((group_spans, rows // group_spans, audio_width), half_type),
+            pltpu.VMEM((audio_width, cols), half_type),
+            pltpu.VMEM((1, cols), full_type),
+            pltpu.VMEM((nc, 1, cols), full_type),
+            pltpu.VMEM((rows, HEAD), full_type),
+            pltpu.VMEM((rows, HEAD), full_type),
+            pltpu.VMEM((2, nx * rows, depth), half_type),
             pltpu.VMEM((nc,) + block, half_type),
             pltpu.VMEM((nc,) + block, half_type),
             pltpu.VMEM((nc,) + block, half_type),
@@ -512,16 +536,16 @@
             pltpu.VMEM(block, full_type),
             pltpu.VMEM((rows, HEAD), full_type),
             pltpu.VMEM(block, half_type),
-            dma(4),
+            dma(8),
             dma(nz), dma(nz), dma(nz), dma(nz), dma(nc), dma(nc),
-            dma(nx), dma(nx), dma(nx), dma(nx),
+            dma(3 * nx), dma(3 * nx), dma(3 * nx), dma(3 * nx),
             dma(nz), dma(nz), dma(nz), dma(nz),
             dma(nx), dma(nx), dma(nx), dma(nx),
             dma(nz), dma(nz), dma(nz), dma(nz), dma(nz), dma(nz), dma(nz), dma(nz),
             dma(nz), dma(nz), dma(nz), dma(nz),
         ],
         compiler_params=pltpu.CompilerParams(
-            collective_id=0, has_side_effects=True, vmem_limit_bytes=48 * 1024 * 1024
+            collective_id=0, has_side_effects=True, vmem_limit_bytes=60 * 1024 * 1024
         ),
         cost_estimate=pl.CostEstimate(
             flops=8 * rows * depth * 3 * cols,
@@ -529,8 +553,9 @@
             transcendentals=0,
         ),
     )(
-        ordered, adapter_weight, adapter_bias.reshape(1, cols), norm_gain.reshape(nc, 1, cols),
-        cosines, sines, live,
+        span_source, lengths,
+        frames.reshape(group_spans, rows // group_spans, audio_width), adapter_weight,
+        adapter_bias.reshape(1, cols), norm_gain.reshape(nc, 1, cols),
         jnp.transpose(qkv_weight, (1, 0, 2)), out_weight, k_cache, v_cache,
     )
 

time: 114 us -> 99.4 us (0.87)
  Pallas kernels: 101 us -> 93.2 us
  local copies, waits for them, and re-layouts: 9.1 us -> 4.7 us
  other arithmetic: 2.54 us -> 0 us
    pallas_call x1, Pallas kernels: 101 us -> 93.2 us  [shards(): pl.pallas_call(functools.partial(layer_kernel, nc, nw, meets, hist), out_...]
    unnamed x15 -> x3, local copies, waits for them, and re-layouts: 8.45 us -> 4.7 us
    convert_element_type x2 -> x0, other arithmetic: 1.46 us -> none  [the longest x1 0.73 us: shards(): angle = positions.astype(jnp.float32)[:, None] * freq[None, :]]
where the time goes in v2:
time: 99.4 us; the launch traced here: 98.5 us
  Pallas kernels  93.2 us (94%)
  local copies, waits for them, and re-layouts  4.7 us (5%)
    pallas_call x1, Pallas kernels, shards(): pl.pallas_call(functools.partial(layer_kernel, nc, nw, meets, hist), out_...  93.2 us
    unnamed x3, local copies, waits for them, and re-layouts  4.7 us

profile of v2, /device:TPU:0, one launch (start us, length us, event | category | flops | bytes accessed | tf_op | source)
XLA Modules:
  0.0 98.5 jit_solution(10067957194977579860)
XLA Ops:
  0.6 93.2 %shard_map.121 = (bf16[128,512]{1,0:T(8,128)(2,1)}, bf16[128,512]{1,0:T(8,128)(2,1)}, bf16[128,512]{1,0:T(8,128)(2,1)}) custom-call(s32[8]{0:T(128)} %source_ref.1, s32[2]{0:T(128)} %lengths_ref.1, bf16[8,16,1280]{2,1,0:T(8,128)(2,1)} %bitcast.5, bf16[1280,512]{1,0:T(8,128)(2,1)} %adapter_hbm.1, f32[1,512]{1,0:T(1,128)} %bitcast.7, f32[8,1,512]{2,1,0:T(1,128)} %bitcast.6, ...), custom_call_target="tpu_custom_call" | custom-call | flops 1610612736 | bytes 7340032 | tf_op jit(solution)/shard_map/pallas_call | solution.py:496
  93.8 1.6 %copy.16 = bf16[128,512]{1,0:T(8,128)(2,1)} copy(bf16[128,512]{1,0:T(8,128)(2,1)} %get-tuple-element.6) | data formatting | bytes 262144
  95.4 1.6 %copy.17 = bf16[128,512]{1,0:T(8,128)(2,1)} copy(bf16[128,512]{1,0:T(8,128)(2,1)} %get-tuple-element.7) | data formatting | bytes 262144
  97.0 1.6 %copy.18 = bf16[128,512]{1,0:T(8,128)(2,1)} copy(bf16[128,512]{1,0:T(8,128)(2,1)} %get-tuple-element.8) | data formatting | bytes 262144

commit v3 on v2

--- a/solution.py
+++ b/solution.py
@@ -25,7 +25,7 @@
     num_own, num_send, num_in, num_cross_send, num_cross_in,
     stat_own, stat_send, stat_in, stat_cross_send, stat_cross_in,
     sum_own, sum_send, sum_in, sum_cross_send, sum_cross_in,
-    new_num, new_stat, attended,
+    attended,
     local_sem,
     fz_s, fz_r, fy_s, fy_r, fx_s, fx_r,
     pair_s, pair_r, cross_s, cross_r,
@@ -133,6 +133,21 @@
     lanes = lax.broadcasted_iota(jnp.int32, (rows, HEAD), 1)
     tokens = lax.broadcasted_iota(jnp.int32, (rows, HEAD), 0)
 
+    first_z, last_z, odd_z = z == 0, z == nz - 1, lax.rem(z, 2)
+
+    def near(index):
+        if nz != 4:
+            return index
+        second = jnp.where(first_z | last_z, 2, 3)
+        third = jnp.where(first_z, 1, jnp.where(last_z, 3, 2))
+        ranked = jnp.where(index == 1, jnp.where(first_z, 3, 1), jnp.where(index == 2, second, third))
+        return jnp.where(index == 0, 0, ranked)
+
+    def far(index):
+        if nz != 4:
+            return (index + 1) % nz
+        return (2, 1 + 2 * odd_z, 3 - 2 * odd_z, 0)[index]
+
     spread_y(feat, c, 0, fy_s, fy_r)
     spread_z(feat, fz_s, fz_r)
     forward(c)
@@ -145,16 +160,17 @@
     cos_ref[...] = jnp.cos(angle)
     sin_ref[...] = jnp.sin(angle) * jnp.where(lanes < HEAD // 2, -1.0, 1.0)
 
-    for step in range(nz):
-        if step:
-            arrived(feat.at[z_block(step)], fz_s.at[step], fz_r.at[step])
-            spread_y(feat, z_block(step), step, fy_s, fy_r)
-            forward(z_block(step))
-        if step:
-            arrived(feat.at[y_block(step - 1)], fy_s.at[step - 1], fy_r.at[step - 1])
-            forward(y_block(step - 1))
-    arrived(feat.at[y_block(nz - 1)], fy_s.at[nz - 1], fy_r.at[nz - 1])
-    forward(y_block(nz - 1))
+    def take_y(step):
+        arrived(feat.at[y_block(step)], fy_s.at[step], fy_r.at[step])
+        forward(y_block(step))
+
+    for index in range(1, nz):
+        step = near(index)
+        arrived(feat.at[z_block(step)], fz_s.at[step], fz_r.at[step])
+        spread_y(feat, z_block(step), step, fy_s, fy_r)
+        forward(z_block(step))
+        take_y(near(index - 1))
+    take_y(near(nz - 1))
 
     loads[0].wait()
 
@@ -248,12 +264,6 @@
             ow_all.at[w], ow_all.at[w], ow_s.at[step], ow_r.at[step],
             c, up(x, step, nx) * 2 + k,
         )
-
-    for step in range(1, nz):
-        arrived(query_all.at[z_block(step)], qz_s.at[step], qz_r.at[step])
-        spread_y(query_all, z_block(step), step, qy_s, qy_r)
-    key_ref[...] = rotated(projected(1))
-    value_ref[...] = projected(2).astype(jnp.bfloat16)
 
     def attend(query, keys, values, mask, meeting_mask):
         stat = jnp.zeros((rows, HEAD), jnp.float32)
@@ -284,19 +294,6 @@
             numers.append(jnp.concatenate(parts, axis=0))
         return jnp.concatenate(numers, axis=1), stat
 
-    causal = lax.broadcasted_iota(jnp.int32, (new, new), 0) >= lax.broadcasted_iota(
-        jnp.int32, (new, new), 1
-    )
-    new_keys, new_values = key_ref[...], value_ref[...]
-    numer, stat = attend(
-        query_all[c],
-        [new_keys[m * new : (m + 1) * new] for m in range(meets)],
-        [new_values[m * new : (m + 1) * new] for m in range(meets)],
-        causal, False,
-    )
-    new_num[...] = numer
-    new_stat[...] = stat
-
     loads[1].wait()
     loads[2].wait()
 
@@ -340,7 +337,22 @@
         return jnp.concatenate(pieces, axis=1), stat
 
     @pl.loop(0, nz)
-    def _(step):
+    def _(index):
+        step = near(index)
+        numer, stat = history(z_block(step))
+        num_own[step] = numer
+        stat_own[step] = stat
+
+        @pl.when(index < nz - 1)
+        def _():
+            after = near(index + 1)
+            ahead = z_block(after)
+            arrived(query_all.at[ahead], qz_s.at[after], qz_r.at[after])
+            remote(
+                query_all.at[ahead], query_all.at[ahead], qy_s.at[after], qy_r.at[after],
+                sibling_c, w,
+            ).start()
+
         block = y_block(step)
         arrived(query_all.at[block], qy_s.at[step], qy_r.at[step])
         numer, stat = history(block)
@@ -353,35 +365,48 @@
             stat_send.at[step], stat_in.at[step], ty_s.at[step], ty_r.at[step], sibling_c, w
         ).start()
 
-    @pl.loop(0, nz)
-    def _(index):
-        step = lax.rem(index + 1, nz)
+    for index in range(1, nz):
+        step = near(index)
         block = z_block(step)
-        own = history(block)
         arrived(num_in.at[step], ny_s.at[step], ny_r.at[step])
         arrived(stat_in.at[step], ty_s.at[step], ty_r.at[step])
         numer, stat = merge(
-            own, (num_in[step].astype(jnp.float32), unpacked(stat_in[step]))
-        )
-
-        @pl.when(step > 0)
-        def _():
-            num_cross_send[step] = numer.astype(jnp.bfloat16)
-            stat_cross_send[step] = packed(stat)
-            remote(
-                num_cross_send.at[step], num_cross_in.at[step], nz_s.at[step], nz_r.at[step],
-                block, w,
-            ).start()
-            remote(
-                stat_cross_send.at[step], stat_cross_in.at[step], tz_s.at[step], tz_r.at[step],
-                block, w,
-            ).start()
-
-        @pl.when(step == 0)
-        def _():
-            numer_all, stat_all = merge((numer, stat), (new_num[...], new_stat[...]))
-            num_own[...] = numer_all
-            stat_own[...] = stat_all
+            (num_own[step], stat_own[step]),
+            (num_in[step].astype(jnp.float32), unpacked(stat_in[step])),
+        )
+        num_cross_send[step] = numer.astype(jnp.bfloat16)
+        stat_cross_send[step] = packed(stat)
+        send(
+            num_cross_send.at[step], num_cross_in.at[step], nz_s.at[step], nz_r.at[step],
+            block, w,
+        )
+        send(
+            stat_cross_send.at[step], stat_cross_in.at[step], tz_s.at[step], tz_r.at[step],
+            block, w,
+        )
+
+    key_ref[...] = rotated(projected(1))
+    value_ref[...] = projected(2).astype(jnp.bfloat16)
+
+    causal = lax.broadcasted_iota(jnp.int32, (new, new), 0) >= lax.broadcasted_iota(
+        jnp.int32, (new, new), 1
+    )
+    new_keys, new_values = key_ref[...], value_ref[...]
+    numer, stat = attend(
+        query_all[c],
+        [new_keys[m * new : (m + 1) * new] for m in range(meets)],
+        [new_values[m * new : (m + 1) * new] for m in range(meets)],
+        causal, False,
+    )
+    arrived(num_in.at[0], ny_s.at[0], ny_r.at[0])
+    arrived(stat_in.at[0], ty_s.at[0], ty_r.at[0])
+    pair = merge(
+        (num_own[0], stat_own[0]),
+        (num_in[0].astype(jnp.float32), unpacked(stat_in[0])),
+    )
+    numer, stat = merge(pair, (numer, stat))
+    num_own[0] = numer
+    stat_own[0] = stat
 
     for step in range(1, nx):
         origin = down(x, step, nx) * 2 + k
@@ -394,16 +419,16 @@
         arrived(num_cross_in.at[step], nz_s.at[step], nz_r.at[step])
         arrived(stat_cross_in.at[step], tz_s.at[step], tz_r.at[step])
         numer, stat = merge(
-            (num_own[...], stat_own[...]),
+            (num_own[0], stat_own[0]),
             (num_cross_in[step].astype(jnp.float32), unpacked(stat_cross_in[step])),
         )
-        num_own[...] = numer
-        stat_own[...] = stat
-    stat = stat_own[...]
+        num_own[0] = numer
+        stat_own[0] = stat
+    stat = stat_own[0]
     for head in range(heads):
         at = slice(head * HEAD, (head + 1) * HEAD)
         attended[:, at] = (
-            num_own[:, at] / stat[:, heads + head : heads + head + 1]
+            num_own[0, :, at] / stat[:, heads + head : heads + head + 1]
         ).astype(jnp.bfloat16)
 
     arrived(ow_all.at[sibling_w], ow_s.at[0], ow_r.at[0])
@@ -418,32 +443,23 @@
             preferred_element_type=jnp.float32,
         )
 
-    @pl.loop(0, nz)
-    def _(index):
-        step = lax.rem(index + 1, nz)
+    for index in range(nz):
+        step = far(index)
         sum_send[step] = out_term(y_block(step)).astype(jnp.bfloat16)
-        remote(
-            sum_send.at[step], sum_in.at[step], by_s.at[step], by_r.at[step], sibling_c, w
-        ).start()
-
-    @pl.loop(0, nz)
-    def _(index):
-        step = lax.rem(index + 1, nz)
+        send(sum_send.at[step], sum_in.at[step], by_s.at[step], by_r.at[step], sibling_c, w)
+    for index in range(nz):
+        step = far(index)
         block = z_block(step)
         term = out_term(block)
         arrived(sum_in.at[step], by_s.at[step], by_r.at[step])
         term += sum_in[step].astype(jnp.float32)
-
-        @pl.when(step > 0)
-        def _():
+        if index < nz - 1:
             sum_cross_send[step] = term.astype(jnp.bfloat16)
-            remote(
+            send(
                 sum_cross_send.at[step], sum_cross_in.at[step], bz_s.at[step], bz_r.at[step],
                 block, w,
-            ).start()
-
-        @pl.when(step == 0)
-        def _():
+            )
+        else:
             sum_own[...] = term
 
     total = sum_own[...]
@@ -467,11 +483,17 @@
     for step in range(nz):
         left(num_send.at[step], ny_s.at[step], ny_r.at[step])
         left(stat_send.at[step], ty_s.at[step], ty_r.at[step])
-        left(sum_send.at[step], by_s.at[step], by_r.at[step])
         if step:
-            left(num_cross_send.at[step], nz_s.at[step], nz_r.at[step])
-            left(stat_cross_send.at[step], tz_s.at[step], tz_r.at[step])
-            left(sum_cross_send.at[step], bz_s.at[step], bz_r.at[step])
+            left(query_all.at[z_block(step)], qy_s.at[step], qy_r.at[step])
+
+
+def hand_out(first, second, third, one, two, three, sems):
+    pairs = ((first, one), (second, two), (third, three))
+    copies = [pltpu.make_async_copy(*pair, sems.at[i]) for i, pair in enumerate(pairs)]
+    for copy in copies:
+        copy.start()
+    for copy in copies:
+        copy.wait()
 
 
 def shards(
@@ -493,7 +515,7 @@
     block = (rows, cols)
     dma = lambda count: pltpu.SemaphoreType.DMA((count,))
     result = jax.ShapeDtypeStruct(block, half_type)
-    return pl.pallas_call(
+    results = pl.pallas_call(
         functools.partial(layer_kernel, nc, nw, meets, hist),
         out_shape=(result, result, result),
         in_specs=[smem] * 2 + [anywhere] * 8,
@@ -518,12 +540,12 @@
             pltpu.VMEM((nx, 3) + block, half_type),
             pltpu.VMEM((nx, 3) + block, half_type),
             pltpu.VMEM((nx, 3) + block, half_type),
-            pltpu.VMEM(block, full_type),
-            pltpu.VMEM((nz,) + block, half_type),
-            pltpu.VMEM((nz,) + block, half_type),
-            pltpu.VMEM((nz,) + block, half_type),
-            pltpu.VMEM((nz,) + block, half_type),
-            pltpu.VMEM((rows, HEAD), full_type),
+            pltpu.VMEM((nz,) + block, full_type),
+            pltpu.VMEM((nz,) + block, half_type),
+            pltpu.VMEM((nz,) + block, half_type),
+            pltpu.VMEM((nz,) + block, half_type),
+            pltpu.VMEM((nz,) + block, half_type),
+            pltpu.VMEM((nz, rows, HEAD), full_type),
             pltpu.VMEM((nz, short, rows), full_type),
             pltpu.VMEM((nz, short, rows), full_type),
             pltpu.VMEM((nz, short, rows), full_type),
@@ -533,8 +555,6 @@
             pltpu.VMEM((nz,) + block, half_type),
             pltpu.VMEM((nz,) + block, half_type),
             pltpu.VMEM((nz,) + block, half_type),
-            pltpu.VMEM(block, full_type),
-            pltpu.VMEM((rows, HEAD), full_type),
             pltpu.VMEM(block, half_type),
             dma(8),
             dma(nz), dma(nz), dma(nz), dma(nz), dma(nc), dma(nc),
@@ -558,6 +578,14 @@
         adapter_bias.reshape(1, cols), norm_gain.reshape(nc, 1, cols),
         jnp.transpose(qkv_weight, (1, 0, 2)), out_weight, k_cache, v_cache,
     )
+    return pl.pallas_call(
+        hand_out,
+        out_shape=(result, result, result),
+        in_specs=[anywhere] * 3,
+        out_specs=(anywhere,) * 3,
+        scratch_shapes=[dma(3)],
+        compiler_params=pltpu.CompilerParams(vmem_limit_bytes=60 * 1024 * 1024),
+    )(*results)
 
 
 def solution(mesh):

time: 99.4 us -> 109 us (1.097)
  Pallas kernels: 93.2 us -> 109 us
  local copies, waits for them, and re-layouts: 4.7 us -> 0 us
    pallas_call x0 -> x1, Pallas kernels: none -> 13 us  [shards(): pl.pallas_call(hand_out, out_shape=(result, result, result), in_specs=[an...]
    unnamed x3 -> x0, local copies, waits for them, and re-layouts: 4.7 us -> none
    pallas_call x1, Pallas kernels: 93.2 us -> 95.5 us  [shards(): pl.pallas_call(functools.partial(layer_kernel, nc, nw, meets, hist), out_...]
where the time goes in v3:
time: 109 us
  Pallas kernels  109 us (100%)
    pallas_call x1, Pallas kernels, shards(): pl.pallas_call(functools.partial(layer_kernel, nc, nw, meets, hist), out_...  95.5 us
    pallas_call x1, Pallas kernels, shards(): pl.pallas_call(hand_out, out_shape=(result, result, result), in_specs=[an...  13 us

profile of v3, /device:TPU:0, one launch (start us, length us, event | category | flops | bytes accessed | tf_op | source)
XLA Modules:
  0.0 109.2 jit_solution(10551912457099251516)
XLA Ops:
  0.6 95.5 %shard_map.121 = (bf16[128,512]{1,0:T(8,128)(2,1)}, bf16[128,512]{1,0:T(8,128)(2,1)}, bf16[128,512]{1,0:T(8,128)(2,1)}) custom-call(s32[8]{0:T(128)} %source_ref.1, s32[2]{0:T(128)} %lengths_ref.1, bf16[8,16,1280]{2,1,0:T(8,128)(2,1)} %bitcast.5, bf16[1280,512]{1,0:T(8,128)(2,1)} %adapter_hbm.1, f32[1,512]{1,0:T(1,128)} %bitcast.7, f32[8,1,512]{2,1,0:T(1,128)} %bitcast.6, ...), custom_call_target="tpu_custom_call" | custom-call | flops 1610612736 | bytes 7340032 | tf_op jit(solution)/shard_map/pallas_call | solution.py:518
  96.1 13.0 %shard_map.122 = (bf16[128,512]{1,0:T(8,128)(2,1)}, bf16[128,512]{1,0:T(8,128)(2,1)}, bf16[128,512]{1,0:T(8,128)(2,1)}) custom-call(bf16[128,512]{1,0:T(8,128)(2,1)} %get-tuple-element.6.first, bf16[128,512]{1,0:T(8,128)(2,1)} %get-tuple-element.7.second, bf16[128,512]{1,0:T(8,128)(2,1)} %get-tuple-element.8.third), custom_call_target="tpu_custom_call" | custom-call | tf_op jit(solution)/shard_map/pallas_call | solution.py:581
